TPU v7x, 128 devices: a whole 4x4x4 slice. The times are simulated.
128 devices in a mesh: dev: 128 (over z, y, x, core).
Axes of the slice: x: 4, y: 4, z: 4, core: 2. Of those that a mesh axis runs over, the one named last changes fastest.
Arguments:
- leaves: float32 [2, 1000, 59392], P(None, None, 'dev'), may hold values from -6 to 6
- send_slot: int32 [4, 32768], P(None, 'dev'), may hold values from 0 to 128, as said below
- recv_slot: int32 [4, 32768], P(None, 'dev'), may hold values from 0 to 128, as said below
- filter_up: float32 [20, 20], replicated, may hold values from -1 to 1.05
- filter_down: float32 [20, 20], replicated, may hold values from -1 to 1.05
Outputs:
- leaves_out: float32 [2, 1000, 59392], P(None, None, 'dev')
Inputs may be any that keep to these rules, and one draw needn't show every extreme that they name: `send_slot`: for each level and each device's block of 256 entries, every local child 0 .. 127 stands in exactly one slot and all other slots hold 128; the number of children one device sends to one device at one level varies from pair to pair and reaches 2 in every level. `recv_slot`: for each level and each device's block of 256 entries, the slots that its sources fill hold each of 0 .. 127 exactly once, and exactly the empty slots hold 128.
All inputs are finite; a program needn't handle non-finite values.
Results may differ from a plain program's by a relative error of at most 0.0001.
Values sent between devices are 32-bit elements; how exact they have to be, the bound alone decides.
No kernel may reach another device: no remote copies, remote signals or barrier semaphores. Data moves between devices by JAX's collectives and lax.ppermute only.
A program may use at most 128 MiB of HBM per device.

v0:
```python
import functools

import jax
import jax.numpy as jnp
from jax import lax
from jax.experimental import pallas as pl
from jax.experimental.pallas import tpu as pltpu
from jax.sharding import PartitionSpec as P

PER = 128
PARENTS = 16
DEGREE = 10
CELLS = 1000
PLANE = 100
ROWS = 32
SLOTS = 256
LIMIT = 32 * 1024 * 1024
TAKE = 0
PLACE = 4

highest = lax.Precision.HIGHEST
f32 = jnp.float32
bf16 = jnp.bfloat16
VMEM = pl.BlockSpec(memory_space=pltpu.VMEM)
SMEM = pl.BlockSpec(memory_space=pltpu.SMEM)
HBM = pl.BlockSpec(memory_space=pltpu.HBM)
DMA = pltpu.SemaphoreType.DMA


def leaf_range(height):
    if height == 0:
        return (0, PER)
    return (PER + 7 * PARENTS * (height - 1), 7 * PARENTS)


def split(value):
    high = value.astype(bf16)
    return high, (value - high.astype(f32)).astype(bf16)


def product(left, right):
    dot = functools.partial(jnp.dot, preferred_element_type=f32)
    return dot(left[0], right[0]) + (dot(left[0], right[1]) + dot(left[1], right[0]))


def windows(chunks):
    lane = lax.broadcasted_iota(jnp.int32, (ROWS, 128), 1)
    result = []
    for i in range(DEGREE):
        first, offset = divmod(PLANE * i, 128)
        value = chunks[first]
        if offset:
            value = pltpu.roll(value, 128 - offset, 1)
            if offset + PLANE > 128:
                later = pltpu.roll(chunks[first + 1], 128 - offset, 1)
                value = jnp.where(lane < 128 - offset, value, later)
        result.append(value)
    return result


def merge(parts):
    lane = lax.broadcasted_iota(jnp.int32, (ROWS, 128), 1)
    result = []
    for part in range(8):
        value = None
        for i in range(DEGREE):
            start = PLANE * i - 128 * part
            if start >= 128 or start + PLANE <= 0:
                continue
            piece = parts[i]
            if start % 128:
                piece = pltpu.roll(piece, start % 128, 1)
            if value is None:
                value = piece
            else:
                value = jnp.where(lane < start, value, piece)
        if part == 7:
            value = jnp.where(lane < CELLS - 896, value, 0.0)
        result.append(value)
    return result


def pack_rows(rows, start, count, flat_ref):
    for first in range(start, start + count, 8):
        for n in range(2):
            for part in range(8):
                if part < 7:
                    value = rows[n, first : first + 8, 128 * part : 128 * part + 128]
                else:
                    value = rows[n, first : first + 8, 896:CELLS]
                    value = jnp.concatenate([value, jnp.zeros((8, 1024 - CELLS), f32)], axis=1)
                flat_ref[pl.ds(first * 16 + n * 8 + part, 8, stride=16), :] = value


def block(flat, index):
    return flat[index * 16 : index * 16 + 16, :]


def fetch(pairs, sems):
    copies = [pltpu.make_async_copy(source, target, sems.at[i]) for i, (source, target) in enumerate(pairs)]
    for copy in copies:
        copy.start()
    return copies


def first_kernel(send_ref, leaves_ref, out_ref, send, rows, flat, sems):
    quarter = PER // 4
    pairs = [(send_ref, send)]
    for i in range(4):
        span = slice(i * quarter, (i + 1) * quarter)
        pairs.append((leaves_ref.at[:, span, :], rows.at[:, span, :]))
    copies = fetch(pairs, sems)
    for i in range(4):
        copies[i + 1].wait()
        pack_rows(rows, i * quarter, quarter, flat)
    copies[0].wait()
    for slot in range(SLOTS):
        start = pl.multiple_of(jnp.minimum(send[0, slot], PER - 1) * 16, 16)
        out_ref[slot] = flat[pl.ds(start, 16), :]


def rest_kernel(maps, leaves_ref, out_ref, rows, flat, filled, sems):
    number = 7 * PARENTS
    pairs = []
    for i in range(3):
        span = slice(i * number, (i + 1) * number)
        pairs.append((leaves_ref.at[:, PER + i * number : PER + (i + 1) * number, :], rows.at[:, span, :]))
    copies = fetch(pairs, sems)
    outs = []
    for i in range(3):
        copies[i].wait()
        pack_rows(rows, i * number, number, flat)
        for child in range(number):
            filled[i, maps[TAKE + i + 1, PARENTS + child]] = block(flat, i * number + child)
        out = pltpu.make_async_copy(filled.at[i], out_ref.at[i], sems.at[3 + i])
        out.start()
        outs.append(out)
    for out in outs:
        out.wait()


def one_hot(dims, axis, index):
    return (lax.broadcasted_iota(jnp.int32, dims, axis) == index).astype(f32)


def plane_index(dims, axis, size):
    position = lax.broadcasted_iota(jnp.int32, dims, axis)
    w, cell = (position >> 7, position & 127)
    j = (cell * 205) >> 11
    k = cell - DEGREE * j
    if size > DEGREE:
        j, k = (j + DEGREE * (w >> 1), k + DEGREE * (w & 1))
    dead = cell >= PLANE
    return jnp.where(dead, -1, j), jnp.where(dead, -1, k)


def exact(left, right, dims=((1,), (0,))):
    return lax.dot_general(left, right, (dims, ((), ())), precision=highest, preferred_element_type=f32)


def planes(filters, outs, ins):
    rows, columns = ((ins // DEGREE) ** 2 * 128, (outs // DEGREE) ** 2 * 128)
    factors = []
    for left, right in zip(plane_index((rows, ins), 0, ins), plane_index((outs, columns), 1, outs)):
        half = exact(one_hot((rows, ins), 1, left), filters, ((1,), (1,)))
        factors.append(exact(half, one_hot((outs, columns), 0, right)))
    return split(factors[0] * factors[1])


def spread(filters, outs, ins):
    rows, columns = (outs * ROWS, ins * ROWS)
    left = one_hot((rows, outs), 1, lax.broadcasted_iota(jnp.int32, (rows, outs), 0) >> 5)
    right = one_hot((ins, columns), 0, lax.broadcasted_iota(jnp.int32, (ins, columns), 1) >> 5)
    row = lax.broadcasted_iota(jnp.int32, (rows, columns), 0) & (ROWS - 1)
    column = lax.broadcasted_iota(jnp.int32, (rows, columns), 1) & (ROWS - 1)
    return split(jnp.where(row == column, exact(exact(left, filters), right), 0.0))


def weight_kernel(up_ref, down_ref, *out_refs):
    both = exact(down_ref[...], up_ref[...])
    up, down = (up_ref[0:DEGREE, :], down_ref[:, 0:DEGREE])
    sizes = ((up, 10, 20), (both, 20, 20), (down, 20, 10))
    for i, (filters, outs, ins) in enumerate(sizes):
        values = planes(filters, outs, ins) + spread(filters, outs, ins)
        for j, value in enumerate(values):
            out_refs[4 * i + j][...] = value


def window_octants(placed, high_ref, low_ref):
    for octant in range(8):
        chunks = [placed[(octant * 8 + part) * ROWS : (octant * 8 + part + 1) * ROWS, :] for part in range(8)]
        x, w = divmod(octant, 4)
        for i, value in enumerate(windows(chunks)):
            high, low = split(value)
            start = (x * DEGREE + i) * ROWS
            high_ref[start : start + ROWS, w * 128 : w * 128 + 128] = high
            low_ref[start : start + ROWS, w * 128 : w * 128 + 128] = low


def place_children(height, maps, arrived_ref, placed):
    for child in range(PER):
        octant, parent = (child % 8, child // 8)
        slot = maps[PLACE + height, child]
        for n in range(2):
            value = arrived_ref[slot, n * 8 : n * 8 + 8, :]
            placed[pl.ds(octant * 8 * ROWS + n * 16 + parent, 8, stride=ROWS), :] = value


def filtered(data, weights):
    half = product(data, (weights[0][...], weights[1][...]))
    return product((weights[2][...], weights[3][...]), split(half))


def up_kernel(height, arrived_ref, maps_ref, filled_ref, w0, w1, w2, w3, out_ref, corner_ref, high_ref, low_ref, *scratch):
    maps, corner, high, low, placed, blocks, v0, v1, v2, v3, sems = scratch
    weights = (v0, v1, v2, v3)
    pairs = [(maps_ref, maps), (filled_ref.at[height], out_ref)] + list(zip((w0, w1, w2, w3), weights))
    copies = fetch(pairs, sems)
    copies[0].wait()
    place_children(height, maps, arrived_ref, placed)
    window_octants(placed, high, low)
    outs = [pltpu.make_async_copy(high, high_ref, sems.at[6]), pltpu.make_async_copy(low, low_ref, sems.at[7])]
    for out in outs:
        out.start()
    for copy in copies[2:]:
        copy.wait()
    value = filtered((high[...], low[...]), weights)
    corner[...] = value
    out = pltpu.make_async_copy(corner, corner_ref, sems.at[8])
    out.start()
    outs.append(out)
    parts = [value[i * ROWS : (i + 1) * ROWS, :] for i in range(DEGREE)]
    for part, chunk in enumerate(merge(parts)):
        for n in range(2):
            blocks[pl.ds(n * 8 + part, 16, stride=16), :] = chunk[n * 16 : n * 16 + 16]
    copies[1].wait()
    for child in range(PARENTS):
        out_ref[maps[TAKE + height + 1, child]] = block(blocks, child)
    for out in outs:
        out.wait()


def emit(height, maps, refined, blocks, out_ref):
    for octant in range(8):
        x, w = divmod(octant, 4)
        parts = []
        for i in range(DEGREE):
            start = (x * DEGREE + i) * ROWS
            parts.append(refined[start : start + ROWS, w * 128 : w * 128 + 128])
        for part, value in enumerate(merge(parts)):
            for n in range(2):
                blocks[pl.ds(octant * 16 + n * 8 + part, 16, stride=128), :] = value[n * 16 : n * 16 + 16]
    for child in range(PER):
        out_ref[maps[PLACE + height, child]] = block(blocks, child)


def top_kernel(height, arrived_ref, maps_ref, w0, w1, w2, w3, out_ref, *scratch):
    maps, high, low, placed, refined, blocks, v0, v1, v2, v3, sems = scratch
    weights = (v0, v1, v2, v3)
    copies = fetch([(maps_ref, maps)] + list(zip((w0, w1, w2, w3), weights)), sems)
    copies[0].wait()
    place_children(height, maps, arrived_ref, placed)
    window_octants(placed, high, low)
    for copy in copies[1:]:
        copy.wait()
    refined[...] = filtered((high[...], low[...]), weights)
    emit(height, maps, refined, blocks, out_ref)


def base_kernel(*refs):
    sources, w, out_ref = (refs[0:6], refs[6:10], refs[10])
    data, weights, refined, sems = (refs[11:17], refs[17:21], refs[21], refs[22])
    copies = fetch(list(zip(tuple(w) + tuple(sources), tuple(weights) + tuple(data))), sems)
    for copy in copies[:4]:
        copy.wait()
    outs = []
    for i in range(3):
        copies[4 + 2 * i].wait()
        copies[5 + 2 * i].wait()
        refined[i] = filtered((data[2 * i][...], data[2 * i + 1][...]), weights)
        out = pltpu.make_async_copy(refined.at[i], out_ref.at[i], sems.at[10 + i])
        out.start()
        outs.append(out)
    for out in outs:
        out.wait()


def down_kernel(height, returned_ref, maps_ref, corner_ref, base_ref, w0, w1, w2, w3, out_ref, *scratch):
    maps, corner, base, placed, delta, refined, blocks, v0, v1, v2, v3, sems = scratch
    weights = (v0, v1, v2, v3)
    pairs = [(maps_ref, maps), (corner_ref, corner)] + list(zip((w0, w1, w2, w3), weights)) + [(base_ref.at[height], base)]
    copies = fetch(pairs, sems)
    copies[0].wait()
    for child in range(PARENTS):
        slot = maps[TAKE + height + 1, child]
        for n in range(2):
            placed[pl.ds(n * 16 + child, 8, stride=ROWS), :] = returned_ref[slot, n * 8 : n * 8 + 8, :]
    lane = lax.broadcasted_iota(jnp.int32, (ROWS, 128), 1)
    chunks = [placed[part * ROWS : (part + 1) * ROWS, :] for part in range(8)]
    copies[1].wait()
    for i, value in enumerate(windows(chunks)):
        change = value - corner[i * ROWS : (i + 1) * ROWS, :]
        delta[i * ROWS : (i + 1) * ROWS, :] = jnp.where(lane < PLANE, change, 0.0)
    for copy in copies[2:]:
        copy.wait()
    refined[...] = base[...] + filtered(split(delta[...]), weights)
    emit(height, maps, refined, blocks, out_ref)


def store_kernel(height, returned_ref, maps_ref, *rest):
    out_ref, maps, flat, rows, sems = rest[-5:]
    start, number = leaf_range(height)
    skip = PER - number
    copy = fetch([(maps_ref, maps)], sems)[0]
    copy.wait()
    outs = []
    step = 16
    for base in range(0, number, step):
        for child in range(base, base + step):
            flat[child * 16 : child * 16 + 16, :] = returned_ref[maps[TAKE + height, child + skip]]
        for first in range(base, base + step, 8):
            for n in range(2):
                for part in range(8):
                    value = flat[pl.ds(first * 16 + n * 8 + part, 8, stride=16), :]
                    if part < 7:
                        rows[n, first : first + 8, 128 * part : 128 * part + 128] = value
                    else:
                        rows[n, first : first + 8, 896:CELLS] = value[:, : CELLS - 896]
        span = slice(base, base + step)
        target = out_ref.at[:, start + base : start + base + step, :]
        out = pltpu.make_async_copy(rows.at[:, span, :], target, sems.at[1 + base // step])
        out.start()
        outs.append(out)
    for out in outs:
        out.wait()


def shape(*dims, dtype=f32):
    return jax.ShapeDtypeStruct(dims, dtype)


def call(kernel, out_shape, in_specs, out_specs, scratch, operands, flops, name, aliases=None):
    moved = sum(4 * one.size for one in operands)
    return pl.pallas_call(
        kernel,
        out_shape=out_shape,
        in_specs=in_specs,
        out_specs=out_specs,
        scratch_shapes=scratch,
        input_output_aliases=aliases or {},
        compiler_params=pltpu.CompilerParams(vmem_limit_bytes=LIMIT),
        cost_estimate=pl.CostEstimate(flops=flops, bytes_accessed=moved, transcendentals=0),
        name=name,
    )(*operands)


def invert(mapping):
    match = mapping[:, None, :] == jnp.arange(PER, dtype=jnp.int32)[None, :, None]
    return jnp.sum(jnp.where(match, jnp.arange(mapping.shape[1], dtype=jnp.int32)[None, None, :], 0), axis=2)


def exchange(blocks):
    return lax.all_to_all(blocks, "dev", split_axis=0, concat_axis=0, tiled=True)


def transform(leaves, send_slot, recv_slot, filter_up, filter_down):
    levels = send_slot.shape[0]
    rows = jnp.swapaxes(leaves, 1, 2)
    slots = shape(SLOTS, 16, 128)
    flat = lambda count: pltpu.VMEM((count * 16, 128), f32)
    sizes = lambda weights: [pltpu.VMEM(one.shape, bf16) for one in weights]
    going = call(
        first_kernel,
        slots,
        [HBM, HBM],
        VMEM,
        [pltpu.SMEM(send_slot.shape, jnp.int32), pltpu.VMEM((2, PER, CELLS), f32), flat(PER), DMA((5,))],
        (send_slot, rows),
        0,
        "pack_first",
    )
    arrived = exchange(going)
    maps = jnp.concatenate([invert(send_slot), invert(recv_slot)], axis=0)
    maps_smem = pltpu.SMEM(maps.shape, jnp.int32)
    filled = call(
        rest_kernel,
        shape(3, SLOTS, 16, 128),
        [SMEM, HBM],
        HBM,
        [pltpu.VMEM((2, 336, CELLS), f32), flat(336), pltpu.VMEM((3, SLOTS, 16, 128), f32), DMA((6,))],
        (maps, rows),
        0,
        "pack_rest",
    )
    halves = lambda *dims: [shape(*dims, dtype=bf16)] * 2
    pieces = halves(512, 128) + halves(320, 640) + halves(512, 512) + halves(640, 640) + halves(128, 512) + halves(640, 320)
    weights = call(weight_kernel, pieces, [VMEM, VMEM], [VMEM] * 12, [], (filter_up, filter_down), 50_000_000, "weights")
    weights = tuple(weights)
    up, both, down = (weights[0:4], weights[4:8], weights[8:12])
    wide = (640, 512)
    placed = pltpu.VMEM((8 * 8 * ROWS, 128), f32)
    split_wide = [pltpu.VMEM(wide, bf16)] * 2
    corners = []
    splits = []
    for height in range(levels - 1):
        going, corner, high, low = call(
            functools.partial(up_kernel, height),
            (slots, shape(320, 128), shape(*wide, dtype=bf16), shape(*wide, dtype=bf16)),
            [VMEM] + [HBM] * 6,
            (VMEM, HBM, HBM, HBM),
            [maps_smem, pltpu.VMEM((320, 128), f32)] + split_wide + [placed, flat(PARENTS)] + sizes(up) + [DMA((9,))],
            (arrived, maps, filled) + up,
            600_000_000,
            "up",
        )
        arrived = exchange(going)
        corners.append(corner)
        splits += [high, low]
    bases = call(
        base_kernel,
        shape(3, *wide),
        [HBM] * 10,
        HBM,
        split_wide * 3 + sizes(both) + [pltpu.VMEM((3, *wide), f32), DMA((13,))],
        tuple(splits) + both,
        7_200_000_000,
        "base",
    )
    height = levels - 1
    going = call(
        functools.partial(top_kernel, height),
        slots,
        [VMEM] + [HBM] * 5,
        VMEM,
        [maps_smem] + split_wide + [placed, pltpu.VMEM(wide, f32), flat(PER)] + sizes(both) + [DMA((5,))],
        (arrived, maps) + both,
        2_400_000_000,
        "top",
    )
    result = None
    while True:
        returned = exchange(going)
        start, number = leaf_range(height)
        final = shape(2, PER + 336, CELLS)
        scratch = [maps_smem, flat(number), pltpu.VMEM((2, number, CELLS), f32), DMA((1 + number // 16,))]
        kernel = functools.partial(store_kernel, height)
        if result is None:
            result = call(kernel, final, [VMEM, HBM], HBM, scratch, (returned, maps), 0, "store")
        else:
            result = call(kernel, final, [VMEM, HBM, HBM], HBM, scratch, (returned, maps, result), 0, "store", {2: 0})
        if height == 0:
            break
        height -= 1
        going = call(
            functools.partial(down_kernel, height),
            slots,
            [VMEM] + [HBM] * 7,
            VMEM,
            [maps_smem, pltpu.VMEM((320, 128), f32), pltpu.VMEM(wide, f32), pltpu.VMEM((8 * ROWS, 128), f32)]
            + [pltpu.VMEM((320, 128), f32), pltpu.VMEM(wide, f32), flat(PER)]
            + sizes(down)
            + [DMA((7,))],
            (returned, maps, corners[height], bases) + down,
            800_000_000,
            "down",
        )
    return jnp.swapaxes(result, 1, 2)


def solution(mesh):
    in_specs = (P(None, None, "dev"), P(None, "dev"), P(None, "dev"), P(), P())
    out_specs = P(None, None, "dev")
    return jax.shard_map(transform, mesh=mesh, in_specs=in_specs, out_specs=out_specs, check_vma=False)
```

profile of v0, /device:TPU:1, one launch (start us, length us, event | category | flops | bytes accessed | tf_op | source)
XLA Modules:
  0.0 342.4 jit_solution(14233141960018799229)
XLA Ops:
  0.0 2.1 copy-done.8
  2.8 2.3 pack_first.1
  5.1 11.5 %all-to-all-start = ((f32[256,16,128]{2,1,0:T(8,128)}), f32[256,16,128]{2,1,0:T(8,128)S(1)}, u32[]{:S(2)}, u32[]{:S(2)}) async-start(f32[256,16,128]{2,1,0:T(8,128)} %pack_first.1), calls=%async_computation | async-start | bytes 4194304 | tf_op jit(solution)/shard_map/all_to_all | solution.py:363
  16.9 2.1 copy-done.9
  18.9 2.6 pack_rest.1.filled_ref
  21.6 2.6 copy-done
  24.2 9.0 %weights.1 = (bf16[512,128]{1,0:T(8,128)(2,1)S(1)}, bf16[512,128]{1,0:T(8,128)(2,1)S(1)}, bf16[320,640]{1,0:T(8,128)(2,1)S(1)}, bf16[320,640]{1,0:T(8,128)(2,1)S...) custom-call(f32[20,20]{1,0:T(8,128)S(1)} %copy-done.45, ...), custom_call_target="tpu_custom_call" | custom-call | flops 50000000 | bytes 3200 | tf_op jit(solution)/shard_map/weights/pallas_call | solution.py:344
  40.1 7.1 %all-to-all-done.arrived_ref = f32[256,16,128]{2,1,0:T(8,128)S(1)} async-done(((f32[256,16,128]{2,1,0:T(8,128)}), f32[256,16,128]{2,1,0:T(8,128)S(1)}, u32[]{:S(2)}, u32[]{:S(2)}) %all-to-all-start) | async-done | bytes 2097184 | tf_op jit(solution)/shard_map/all_to_all | solution.py:363
  47.1 2.8 copy-done.1
  52.7 4.4 %up.3 = (f32[256,16,128]{2,1,0:T(8,128)S(1)}, f32[320,128]{1,0:T(8,128)S(1)}, bf16[640,512]{1,0:T(8,128)(2,1)S(1)}, bf16[640,512]{1,0:T(8,128)(2,1)S(1)}) custom-call(f32[256,16,128]{2,1,0:T(8,128)S(1)} %all-to-all-done.arrived_ref, s32[8,128]{1,0:T(8,128)S(1)} %pad_add_fusion.maps.maps_ref, f32[3,256,16,128]{3,2,1,0:T(8,128)S(1)} %copy-done.1, ...), custom_call_target="tpu_custom_call" | custom-call | flops 600000000 | bytes 10555392 | tf_op jit(solution)/shard_map/up/pallas_call | solution.py:344
  59.6 34.5 %all_to_all.40.arrived_ref = f32[256,16,128]{2,1,0:T(8,128)S(1)} all-to-all(f32[256,16,128]{2,1,0:T(8,128)S(1)} %get-tuple-element.33), channel_id=1, replica_groups=mesh['dev'=128] {'dev'}, dimensions={0} | all-to-all | bytes 4194304 | tf_op jit(solution)/shard_map/all_to_all | solution.py:363
  94.1 4.4 %up.4 = (f32[256,16,128]{2,1,0:T(8,128)S(1)}, f32[320,128]{1,0:T(8,128)S(1)}, bf16[640,512]{1,0:T(8,128)(2,1)S(1)}, bf16[640,512]{1,0:T(8,128)(2,1)S(1)}) custom-call(f32[256,16,128]{2,1,0:T(8,128)S(1)} %all_to_all.40.arrived_ref, s32[8,128]{1,0:T(8,128)S(1)} %pad_add_fusion.maps.maps_ref, f32[3,256,16,128]{3,2,1,0:T(8,128)S(1)} %copy-done.1, ...), custom_call_target="tpu_custom_call" | custom-call | flops 600000000 | bytes 10555392 | tf_op jit(solution)/shard_map/up/pallas_call | solution.py:344
  100.9 34.4 %all_to_all.41.arrived_ref = f32[256,16,128]{2,1,0:T(8,128)S(1)} all-to-all(f32[256,16,128]{2,1,0:T(8,128)S(1)} %get-tuple-element.34), channel_id=1, replica_groups=mesh['dev'=128] {'dev'}, dimensions={0} | all-to-all | bytes 4194304 | tf_op jit(solution)/shard_map/all_to_all | solution.py:363
  135.2 4.4 %up.5 = (f32[256,16,128]{2,1,0:T(8,128)S(1)}, f32[320,128]{1,0:T(8,128)S(1)}, bf16[640,512]{1,0:T(8,128)(2,1)S(1)}, bf16[640,512]{1,0:T(8,128)(2,1)S(1)}) custom-call(f32[256,16,128]{2,1,0:T(8,128)S(1)} %all_to_all.41.arrived_ref, s32[8,128]{1,0:T(8,128)S(1)} %pad_add_fusion.maps.maps_ref, f32[3,256,16,128]{3,2,1,0:T(8,128)S(1)} %copy-done.1, ...), custom_call_target="tpu_custom_call" | custom-call | flops 600000000 | bytes 10555392 | tf_op jit(solution)/shard_map/up/pallas_call | solution.py:344
  139.7 34.6 %all_to_all.42.arrived_ref = f32[256,16,128]{2,1,0:T(8,128)S(1)} all-to-all(f32[256,16,128]{2,1,0:T(8,128)S(1)} %get-tuple-element.35), channel_id=1, replica_groups=mesh['dev'=128] {'dev'}, dimensions={0} | all-to-all | bytes 4194304 | tf_op jit(solution)/shard_map/all_to_all | solution.py:363
  174.4 5.4 %top.1 = f32[256,16,128]{2,1,0:T(8,128)S(1)} custom-call(f32[256,16,128]{2,1,0:T(8,128)S(1)} %all_to_all.42.arrived_ref, s32[8,128]{1,0:T(8,128)S(1)} %pad_add_fusion.maps.maps_ref, bf16[512,512]{1,0:T(8,128)(2,1)S(1)} %copy-done.54, bf16[512,512]{1,0:T(8,128)(2,1)S(1)} %copy-done.57, bf16[640,640]{1,0:T(8,128)(2,1)S(1)} %copy-done.48, ...), custom_call_target="tpu_custom_call" | custom-call | flops 2400000000 | bytes 7475200 | tf_op jit(solution)/shard_map/top/pallas_call | solution.py:344
  181.1 4.4 %all-to-all-start.4 = ((f32[256,16,128]{2,1,0:T(8,128)}), f32[256,16,128]{2,1,0:T(8,128)S(1)}, u32[]{:S(2)}, u32[]{:S(2)}) async-start(f32[256,16,128]{2,1,0:T(8,128)} %copy-done.14), calls=%async_computation.4 | async-start | bytes 4194304 | tf_op jit(solution)/shard_map/all_to_all | solution.py:363
  196.4 10.1 %base.1.base_ref = f32[3,640,512]{2,1,0:T(8,128)S(1)} custom-call(bf16[640,512]{1,0:T(8,128)(2,1)S(1)} %copy-done.34, bf16[640,512]{1,0:T(8,128)(2,1)S(1)} %copy-done.36, bf16[640,512]{1,0:T(8,128)(2,1)S(1)} %copy-done.38, bf16[640,512]{1,0:T(8,128)(2,1)S(1)} %copy-done.40, bf16[640,512]{1,0:T(8,128)(2,1)S(1)} %copy-done.42, ...), custom_call_target="tpu_custom_call" | custom-call | flops 7200000000 | bytes 13238272 | tf_op jit(solution)/shard_map/base/pallas_call | solution.py:344
  206.6 1.9 copy-done.2
  208.4 7.8 %all-to-all-done.4.returned_ref = f32[256,16,128]{2,1,0:T(8,128)S(1)} async-done(((f32[256,16,128]{2,1,0:T(8,128)}), f32[256,16,128]{2,1,0:T(8,128)S(1)}, u32[]{:S(2)}, u32[]{:S(2)}) %all-to-all-start.4) | async-done | bytes 2097184 | tf_op jit(solution)/shard_map/all_to_all | solution.py:363
  216.2 2.1 copy-done.3
  219.2 4.0 %down.3 = f32[256,16,128]{2,1,0:T(8,128)S(1)} custom-call(f32[256,16,128]{2,1,0:T(8,128)S(1)} %all-to-all-done.4.returned_ref, s32[8,128]{1,0:T(8,128)S(1)} %pad_add_fusion.maps.maps_ref, f32[320,128]{1,0:T(8,128)S(1)} %copy-done.30, f32[3,640,512]{2,1,0:T(8,128)S(1)} %copy-done.3, bf16[128,512]{1,0:T(8,128)(2,1)S(1)} %copy-done.16, ...), custom_call_target="tpu_custom_call" | custom-call | flops 800000000 | bytes 8359936 | tf_op jit(solution)/shard_map/down/pallas_call | solution.py:344
  223.3 34.5 %all_to_all.43.returned_ref = f32[256,16,128]{2,1,0:T(8,128)S(1)} all-to-all(f32[256,16,128]{2,1,0:T(8,128)S(1)} %down.3), channel_id=1, replica_groups=mesh['dev'=128] {'dev'}, dimensions={0} | all-to-all | bytes 4194304 | tf_op jit(solution)/shard_map/all_to_all | solution.py:363
  257.8 4.0 %down.4 = f32[256,16,128]{2,1,0:T(8,128)S(1)} custom-call(f32[256,16,128]{2,1,0:T(8,128)S(1)} %all_to_all.43.returned_ref, s32[8,128]{1,0:T(8,128)S(1)} %pad_add_fusion.maps.maps_ref, f32[320,128]{1,0:T(8,128)S(1)} %copy-done.28, f32[3,640,512]{2,1,0:T(8,128)S(1)} %copy-done.3, bf16[128,512]{1,0:T(8,128)(2,1)S(1)} %copy-done.16, ...), custom_call_target="tpu_custom_call" | custom-call | flops 800000000 | bytes 8359936 | tf_op jit(solution)/shard_map/down/pallas_call | solution.py:344
  261.8 34.5 %all_to_all.44.returned_ref = f32[256,16,128]{2,1,0:T(8,128)S(1)} all-to-all(f32[256,16,128]{2,1,0:T(8,128)S(1)} %down.4), channel_id=1, replica_groups=mesh['dev'=128] {'dev'}, dimensions={0} | all-to-all | bytes 4194304 | tf_op jit(solution)/shard_map/all_to_all | solution.py:363
  296.4 4.0 %down.5 = f32[256,16,128]{2,1,0:T(8,128)S(1)} custom-call(f32[256,16,128]{2,1,0:T(8,128)S(1)} %all_to_all.44.returned_ref, s32[8,128]{1,0:T(8,128)S(1)} %pad_add_fusion.maps.maps_ref, f32[320,128]{1,0:T(8,128)S(1)} %copy-done.26, f32[3,640,512]{2,1,0:T(8,128)S(1)} %copy-done.3, bf16[128,512]{1,0:T(8,128)(2,1)S(1)} %copy-done.16, ...), custom_call_target="tpu_custom_call" | custom-call | flops 800000000 | bytes 8359936 | tf_op jit(solution)/shard_map/down/pallas_call | solution.py:344
  303.1 5.4 %all-to-all-start.7 = ((f32[256,16,128]{2,1,0:T(8,128)}), f32[256,16,128]{2,1,0:T(8,128)}, u32[]{:S(2)}, u32[]{:S(2)}) async-start(f32[256,16,128]{2,1,0:T(8,128)} %copy-done.10), calls=%async_computation.7 | async-start | bytes 4194304 | tf_op jit(solution)/shard_map/all_to_all | solution.py:363
  308.6 1.7 store.4.rest_0_
  310.3 1.7 store.5.rest_0_
  312.0 1.7 store.6.rest_0_
  313.7 25.2 %all-to-all-done.7.returned_ref = f32[256,16,128]{2,1,0:T(8,128)} async-done(((f32[256,16,128]{2,1,0:T(8,128)}), f32[256,16,128]{2,1,0:T(8,128)}, u32[]{:S(2)}, u32[]{:S(2)}) %all-to-all-start.7) | async-done | bytes 2097184 | tf_op jit(solution)/shard_map/all_to_all | solution.py:363
  338.9 3.3 store.7
  (116 shorter events, 31.2 us)
Async XLA Ops:
  0.0 2.1 copy-start.8
  5.1 11.5 %copy-start.32 = (s32[4,256]{1,0:T(4,128)S(1)}, s32[4,256]{1,0:T(4,128)}, u32[]{:S(2)}) copy-start(s32[4,256]{1,0:T(4,128)} %send_ref.1) | copy-start | bytes 12292
  5.1 11.5 %copy-start.59 = (s32[4,256]{1,0:T(4,128)S(1)}, s32[4,256]{1,0:T(4,128)}, u32[]{:S(2)}) copy-start(s32[4,256]{1,0:T(4,128)} %param.7) | copy-start | bytes 12292
  5.1 42.0 %all-to-all-start = ((f32[256,16,128]{2,1,0:T(8,128)}), f32[256,16,128]{2,1,0:T(8,128)S(1)}, u32[]{:S(2)}, u32[]{:S(2)}) async-start(f32[256,16,128]{2,1,0:T(8,128)} %pack_first.1), calls=%async_computation | async-start | bytes 4194304 | tf_op jit(solution)/shard_map/all_to_all | solution.py:363
  16.9 2.1 copy-start.9
  18.9 5.3 %copy-start.45 = (f32[20,20]{1,0:T(8,128)S(1)}, f32[20,20]{1,0:T(8,128)}, u32[]{:S(2)}) copy-start(f32[20,20]{1,0:T(8,128)} %up_ref.1) | copy-start | bytes 4804
  18.9 5.3 %copy-start.46 = (f32[20,20]{1,0:T(8,128)S(1)}, f32[20,20]{1,0:T(8,128)}, u32[]{:S(2)}) copy-start(f32[20,20]{1,0:T(8,128)} %down_ref.1) | copy-start | bytes 4804
  21.6 2.6 copy-start
  47.1 2.8 copy-start.1
  59.6 34.5 %copy-start.13 = (bf16[320,640]{1,0:T(8,128)(2,1)S(1)}, bf16[320,640]{1,0:T(8,128)(2,1)}, u32[]{:S(2)}) copy-start(bf16[320,640]{1,0:T(8,128)(2,1)} %copy-done.11) | copy-start | bytes 1228804
  59.6 34.5 %copy-start.21 = (bf16[512,128]{1,0:T(8,128)(2,1)S(1)}, bf16[512,128]{1,0:T(8,128)(2,1)}, u32[]{:S(2)}) copy-start(bf16[512,128]{1,0:T(8,128)(2,1)} %copy-done.19) | copy-start | bytes 393220
  59.6 34.5 %copy-start.24 = (bf16[512,128]{1,0:T(8,128)(2,1)S(1)}, bf16[512,128]{1,0:T(8,128)(2,1)}, u32[]{:S(2)}) copy-start(bf16[512,128]{1,0:T(8,128)(2,1)} %copy-done.22) | copy-start | bytes 393220
  139.7 34.7 %copy-start.29 = (f32[320,128]{1,0:T(8,128)}, f32[320,128]{1,0:T(8,128)S(1)}, u32[]{:S(2)}) copy-start(f32[320,128]{1,0:T(8,128)S(1)} %get-tuple-element.40.corner_ref) | copy-start | bytes 491524
  139.7 34.7 %copy-start.41 = (bf16[640,512]{1,0:T(8,128)(2,1)}, bf16[640,512]{1,0:T(8,128)(2,1)S(1)}, u32[]{:S(2)}) copy-start(bf16[640,512]{1,0:T(8,128)(2,1)S(1)} %get-tuple-element.45.refs_4_) | copy-start | bytes 1966084
  139.7 34.7 %copy-start.43 = (bf16[640,512]{1,0:T(8,128)(2,1)}, bf16[640,512]{1,0:T(8,128)(2,1)S(1)}, u32[]{:S(2)}) copy-start(bf16[640,512]{1,0:T(8,128)(2,1)S(1)} %get-tuple-element.46.refs_5_) | copy-start | bytes 1966084
  139.7 34.7 %copy-start.48 = (bf16[640,640]{1,0:T(8,128)(2,1)S(1)}, bf16[640,640]{1,0:T(8,128)(2,1)}, u32[]{:S(2)}) copy-start(bf16[640,640]{1,0:T(8,128)(2,1)} %copy-done.47) | copy-start | bytes 2457604
  139.7 34.7 %copy-start.51 = (bf16[640,640]{1,0:T(8,128)(2,1)S(1)}, bf16[640,640]{1,0:T(8,128)(2,1)}, u32[]{:S(2)}) copy-start(bf16[640,640]{1,0:T(8,128)(2,1)} %copy-done.50) | copy-start | bytes 2457604
  139.7 34.7 %copy-start.54 = (bf16[512,512]{1,0:T(8,128)(2,1)S(1)}, bf16[512,512]{1,0:T(8,128)(2,1)}, u32[]{:S(2)}) copy-start(bf16[512,512]{1,0:T(8,128)(2,1)} %copy-done.53) | copy-start | bytes 1572868
  139.7 34.7 %copy-start.57 = (bf16[512,512]{1,0:T(8,128)(2,1)S(1)}, bf16[512,512]{1,0:T(8,128)(2,1)}, u32[]{:S(2)}) copy-start(bf16[512,512]{1,0:T(8,128)(2,1)} %copy-done.56) | copy-start | bytes 1572868
  181.1 35.0 %all-to-all-start.4 = ((f32[256,16,128]{2,1,0:T(8,128)}), f32[256,16,128]{2,1,0:T(8,128)S(1)}, u32[]{:S(2)}, u32[]{:S(2)}) async-start(f32[256,16,128]{2,1,0:T(8,128)} %copy-done.14), calls=%async_computation.4 | async-start | bytes 4194304 | tf_op jit(solution)/shard_map/all_to_all | solution.py:363
  196.4 19.8 %copy-start.16 = (bf16[128,512]{1,0:T(8,128)(2,1)S(1)}, bf16[128,512]{1,0:T(8,128)(2,1)}, u32[]{:S(2)}) copy-start(bf16[128,512]{1,0:T(8,128)(2,1)} %copy-done.15) | copy-start | bytes 393220
  196.4 19.8 %copy-start.18 = (bf16[128,512]{1,0:T(8,128)(2,1)S(1)}, bf16[128,512]{1,0:T(8,128)(2,1)}, u32[]{:S(2)}) copy-start(bf16[128,512]{1,0:T(8,128)(2,1)} %copy-done.17) | copy-start | bytes 393220
  206.6 1.9 copy-start.2
  216.2 2.1 copy-start.3
  223.2 34.5 %copy-start.28 = (f32[320,128]{1,0:T(8,128)S(1)}, f32[320,128]{1,0:T(8,128)}, u32[]{:S(2)}) copy-start(f32[320,128]{1,0:T(8,128)} %copy-done.27) | copy-start | bytes 491524
  257.8 4.0 %copy-start.4 = (f32[256,16,128]{2,1,0:T(8,128)}, f32[256,16,128]{2,1,0:T(8,128)S(1)}, u32[]{:S(2)}) copy-start(f32[256,16,128]{2,1,0:T(8,128)S(1)} %all_to_all.43.returned_ref) | copy-start | bytes 6291460
  261.8 34.5 %copy-start.26 = (f32[320,128]{1,0:T(8,128)S(1)}, f32[320,128]{1,0:T(8,128)}, u32[]{:S(2)}) copy-start(f32[320,128]{1,0:T(8,128)} %copy-done.25) | copy-start | bytes 491524
  300.4 1.4 copy-start.6
  301.8 1.4 copy-start.10
  303.1 35.7 %all-to-all-start.7 = ((f32[256,16,128]{2,1,0:T(8,128)}), f32[256,16,128]{2,1,0:T(8,128)}, u32[]{:S(2)}, u32[]{:S(2)}) async-start(f32[256,16,128]{2,1,0:T(8,128)} %copy-done.10), calls=%async_computation.7 | async-start | bytes 4194304 | tf_op jit(solution)/shard_map/all_to_all | solution.py:363
  308.6 1.7 copy-start.5
  310.3 1.7 copy-start.7
  (31 other events, 28.2 us)
where the time goes:
time: 344 us; the launch traced here: 342 us
  blocking collectives  173 us (50%)
  Pallas kernels  63.2 us (18%)
  local copies, waits for them, and re-layouts  44.6 us (13%)
  waiting for transfers between devices  40 us (12%)
  starting transfers between devices  21.3 us (6%)
    all_to_all x5, blocking collectives, exchange(): lax.all_to_all(blocks, 'dev', split_axis=0, concat_axis=0, tiled=True)  173 us
    pallas_call x15, Pallas kernels, call(): pl.pallas_call(kernel, out_shape=out_shape, in_specs=in_specs, out_specs=...  63.2 us
    unnamed x120, local copies, waits for them, and re-layouts  44.6 us
    all_to_all x3, waiting for transfers between devices, exchange(): lax.all_to_all(blocks, 'dev', split_axis=0, concat_axis=0, tiled=True)  40 us
    all_to_all x3, starting transfers between devices, exchange(): lax.all_to_all(blocks, 'dev', split_axis=0, concat_axis=0, tiled=True)  21.3 us
  transfers between devices with their start and end apart: 3, of which 3 were waited for; matrix products, arithmetic and copies ran while one was open for 0% of the time, Pallas kernels for 8%

commit v1 on v0

--- a/solution.py
+++ b/solution.py
@@ -14,7 +14,11 @@
 PLANE = 100
 ROWS = 32
 SLOTS = 256
-LIMIT = 32 * 1024 * 1024
+LIMIT = 42_000_000
+FULL = 63_400_000
+UP_ROW, BOTH_ROW, DOWN_ROW, PLANE_ROW, DOWN_PLANE, SPLIT = (0, 640, 1920, 3200, 4224, 4480)
+BANK = 16384
+CORNER = 20
 TAKE = 0
 PLACE = 4
 
@@ -132,7 +136,7 @@
         pack_rows(rows, i * number, number, flat)
         for child in range(number):
             filled[i, maps[TAKE + i + 1, PARENTS + child]] = block(flat, i * number + child)
-        out = pltpu.make_async_copy(filled.at[i], out_ref.at[i], sems.at[3 + i])
+        out = pltpu.make_async_copy(filled.at[i], out_ref.at[i, 0:SLOTS], sems.at[3 + i])
         out.start()
         outs.append(out)
     for out in outs:
@@ -176,14 +180,39 @@
     return split(jnp.where(row == column, exact(exact(left, filters), right), 0.0))
 
 
-def weight_kernel(up_ref, down_ref, *out_refs):
+def weight_kernel(up_ref, down_ref, bank_ref, bank, sem):
     both = exact(down_ref[...], up_ref[...])
     up, down = (up_ref[0:DEGREE, :], down_ref[:, 0:DEGREE])
-    sizes = ((up, 10, 20), (both, 20, 20), (down, 20, 10))
-    for i, (filters, outs, ins) in enumerate(sizes):
-        values = planes(filters, outs, ins) + spread(filters, outs, ins)
-        for j, value in enumerate(values):
-            out_refs[4 * i + j][...] = value
+    for i in range(2):
+        bank[PLANE_ROW + 512 * i : PLANE_ROW + 512 * (i + 1), 512:640] = planes(up, 10, 20)[i]
+        bank[PLANE_ROW + 512 * i : PLANE_ROW + 512 * (i + 1), 0:512] = planes(both, 20, 20)[i]
+        bank[DOWN_PLANE + 128 * i : DOWN_PLANE + 128 * (i + 1), 0:512] = planes(down, 20, 10)[i]
+        bank[UP_ROW + 320 * i : UP_ROW + 320 * (i + 1), :] = spread(up, 10, 20)[i]
+        bank[BOTH_ROW + 640 * i : BOTH_ROW + 640 * (i + 1), :] = spread(both, 20, 20)[i]
+        bank[DOWN_ROW + 640 * i : DOWN_ROW + 640 * (i + 1), 0:320] = spread(down, 20, 10)[i]
+    copy = pltpu.make_async_copy(bank, bank_ref.at[0:SPLIT, :], sem)
+    copy.start()
+    copy.wait()
+
+
+def section(bank_ref, start, rows, first, columns):
+    return [bank_ref.at[start + i * rows : start + (i + 1) * rows, first : first + columns] for i in range(2)]
+
+
+def up_weights(bank_ref):
+    return section(bank_ref, PLANE_ROW, 512, 512, 128) + section(bank_ref, UP_ROW, 320, 0, 640)
+
+
+def both_weights(bank_ref):
+    return section(bank_ref, PLANE_ROW, 512, 0, 512) + section(bank_ref, BOTH_ROW, 640, 0, 640)
+
+
+def down_weights(bank_ref):
+    return section(bank_ref, DOWN_PLANE, 128, 0, 512) + section(bank_ref, DOWN_ROW, 640, 0, 384)
+
+
+def split_children(bank_ref, height):
+    return section(bank_ref, SPLIT + 1280 * height, 640, 0, 512)
 
 
 def window_octants(placed, high_ref, low_ref):
@@ -208,25 +237,27 @@
 
 def filtered(data, weights):
     half = product(data, (weights[0][...], weights[1][...]))
-    return product((weights[2][...], weights[3][...]), split(half))
-
-
-def up_kernel(height, arrived_ref, maps_ref, filled_ref, w0, w1, w2, w3, out_ref, corner_ref, high_ref, low_ref, *scratch):
+    depth = half.shape[0]
+    return product((weights[2][:, :depth], weights[3][:, :depth]), split(half))
+
+
+def up_kernel(height, arrived_ref, maps_ref, filled_ref, bank_ref, out_ref, state_ref, kept_ref, *scratch):
     maps, corner, high, low, placed, blocks, v0, v1, v2, v3, sems = scratch
     weights = (v0, v1, v2, v3)
-    pairs = [(maps_ref, maps), (filled_ref.at[height], out_ref)] + list(zip((w0, w1, w2, w3), weights))
+    pairs = [(maps_ref, maps), (filled_ref.at[height, 0:SLOTS], out_ref)] + list(zip(up_weights(bank_ref), weights))
     copies = fetch(pairs, sems)
     copies[0].wait()
     place_children(height, maps, arrived_ref, placed)
     window_octants(placed, high, low)
-    outs = [pltpu.make_async_copy(high, high_ref, sems.at[6]), pltpu.make_async_copy(low, low_ref, sems.at[7])]
+    targets = split_children(kept_ref, height)
+    outs = [pltpu.make_async_copy(high, targets[0], sems.at[6]), pltpu.make_async_copy(low, targets[1], sems.at[7])]
     for out in outs:
         out.start()
     for copy in copies[2:]:
         copy.wait()
     value = filtered((high[...], low[...]), weights)
-    corner[...] = value
-    out = pltpu.make_async_copy(corner, corner_ref, sems.at[8])
+    corner[...] = value.reshape(CORNER, 16, 128)
+    out = pltpu.make_async_copy(corner, state_ref.at[height, SLOTS : SLOTS + CORNER], sems.at[8])
     out.start()
     outs.append(out)
     parts = [value[i * ROWS : (i + 1) * ROWS, :] for i in range(DEGREE)]
@@ -254,10 +285,10 @@
         out_ref[maps[PLACE + height, child]] = block(blocks, child)
 
 
-def top_kernel(height, arrived_ref, maps_ref, w0, w1, w2, w3, out_ref, *scratch):
+def top_kernel(height, arrived_ref, maps_ref, bank_ref, out_ref, *scratch):
     maps, high, low, placed, refined, blocks, v0, v1, v2, v3, sems = scratch
     weights = (v0, v1, v2, v3)
-    copies = fetch([(maps_ref, maps)] + list(zip((w0, w1, w2, w3), weights)), sems)
+    copies = fetch([(maps_ref, maps)] + list(zip(both_weights(bank_ref), weights)), sems)
     copies[0].wait()
     place_children(height, maps, arrived_ref, placed)
     window_octants(placed, high, low)
@@ -267,10 +298,12 @@
     emit(height, maps, refined, blocks, out_ref)
 
 
-def base_kernel(*refs):
-    sources, w, out_ref = (refs[0:6], refs[6:10], refs[10])
-    data, weights, refined, sems = (refs[11:17], refs[17:21], refs[21], refs[22])
-    copies = fetch(list(zip(tuple(w) + tuple(sources), tuple(weights) + tuple(data))), sems)
+def base_kernel(bank_ref, out_ref, *scratch):
+    data, weights, refined, sems = (scratch[0:6], scratch[6:10], scratch[10], scratch[11])
+    pairs = list(zip(both_weights(bank_ref), weights))
+    for height in range(3):
+        pairs += list(zip(split_children(bank_ref, height), data[2 * height : 2 * height + 2]))
+    copies = fetch(pairs, sems)
     for copy in copies[:4]:
         copy.wait()
     outs = []
@@ -285,10 +318,11 @@
         out.wait()
 
 
-def down_kernel(height, returned_ref, maps_ref, corner_ref, base_ref, w0, w1, w2, w3, out_ref, *scratch):
+def down_kernel(height, returned_ref, maps_ref, state_ref, base_ref, bank_ref, out_ref, *scratch):
     maps, corner, base, placed, delta, refined, blocks, v0, v1, v2, v3, sems = scratch
     weights = (v0, v1, v2, v3)
-    pairs = [(maps_ref, maps), (corner_ref, corner)] + list(zip((w0, w1, w2, w3), weights)) + [(base_ref.at[height], base)]
+    pairs = [(maps_ref, maps), (state_ref.at[height, SLOTS : SLOTS + CORNER], corner)]
+    pairs += list(zip(down_weights(bank_ref), weights)) + [(base_ref.at[height], base)]
     copies = fetch(pairs, sems)
     copies[0].wait()
     for child in range(PARENTS):
@@ -299,7 +333,7 @@
     chunks = [placed[part * ROWS : (part + 1) * ROWS, :] for part in range(8)]
     copies[1].wait()
     for i, value in enumerate(windows(chunks)):
-        change = value - corner[i * ROWS : (i + 1) * ROWS, :]
+        change = value - corner[2 * i : 2 * i + 2].reshape(ROWS, 128)
         delta[i * ROWS : (i + 1) * ROWS, :] = jnp.where(lane < PLANE, change, 0.0)
     for copy in copies[2:]:
         copy.wait()
@@ -339,7 +373,7 @@
     return jax.ShapeDtypeStruct(dims, dtype)
 
 
-def call(kernel, out_shape, in_specs, out_specs, scratch, operands, flops, name, aliases=None):
+def call(kernel, out_shape, in_specs, out_specs, scratch, operands, flops, name, aliases=None, limit=LIMIT):
     moved = sum(4 * one.size for one in operands)
     return pl.pallas_call(
         kernel,
@@ -348,7 +382,7 @@
         out_specs=out_specs,
         scratch_shapes=scratch,
         input_output_aliases=aliases or {},
-        compiler_params=pltpu.CompilerParams(vmem_limit_bytes=LIMIT),
+        compiler_params=pltpu.CompilerParams(vmem_limit_bytes=limit),
         cost_estimate=pl.CostEstimate(flops=flops, bytes_accessed=moved, transcendentals=0),
         name=name,
     )(*operands)
@@ -368,7 +402,6 @@
     rows = jnp.swapaxes(leaves, 1, 2)
     slots = shape(SLOTS, 16, 128)
     flat = lambda count: pltpu.VMEM((count * 16, 128), f32)
-    sizes = lambda weights: [pltpu.VMEM(one.shape, bf16) for one in weights]
     going = call(
         first_kernel,
         slots,
@@ -378,62 +411,70 @@
         (send_slot, rows),
         0,
         "pack_first",
+        limit=FULL,
     )
     arrived = exchange(going)
     maps = jnp.concatenate([invert(send_slot), invert(recv_slot)], axis=0)
     maps_smem = pltpu.SMEM(maps.shape, jnp.int32)
     filled = call(
         rest_kernel,
-        shape(3, SLOTS, 16, 128),
+        shape(8, SLOTS + CORNER, 16, 128),
         [SMEM, HBM],
         HBM,
         [pltpu.VMEM((2, 336, CELLS), f32), flat(336), pltpu.VMEM((3, SLOTS, 16, 128), f32), DMA((6,))],
         (maps, rows),
         0,
         "pack_rest",
+        limit=FULL,
     )
-    halves = lambda *dims: [shape(*dims, dtype=bf16)] * 2
-    pieces = halves(512, 128) + halves(320, 640) + halves(512, 512) + halves(640, 640) + halves(128, 512) + halves(640, 320)
-    weights = call(weight_kernel, pieces, [VMEM, VMEM], [VMEM] * 12, [], (filter_up, filter_down), 50_000_000, "weights")
-    weights = tuple(weights)
-    up, both, down = (weights[0:4], weights[4:8], weights[8:12])
+    bank = call(
+        weight_kernel,
+        shape(BANK, 640, dtype=bf16),
+        [VMEM, VMEM],
+        HBM,
+        [pltpu.VMEM((SPLIT, 640), bf16), DMA],
+        (filter_up, filter_down),
+        50_000_000,
+        "weights",
+        limit=FULL,
+    )
+    sizes = lambda *dims: [pltpu.VMEM(one, bf16) for one in dims for _ in range(2)]
+    up, both, down = (sizes((512, 128), (320, 640)), sizes((512, 512), (640, 640)), sizes((128, 512), (640, 384)))
     wide = (640, 512)
     placed = pltpu.VMEM((8 * 8 * ROWS, 128), f32)
     split_wide = [pltpu.VMEM(wide, bf16)] * 2
-    corners = []
-    splits = []
     for height in range(levels - 1):
-        going, corner, high, low = call(
+        going, filled, bank = call(
             functools.partial(up_kernel, height),
-            (slots, shape(320, 128), shape(*wide, dtype=bf16), shape(*wide, dtype=bf16)),
-            [VMEM] + [HBM] * 6,
-            (VMEM, HBM, HBM, HBM),
-            [maps_smem, pltpu.VMEM((320, 128), f32)] + split_wide + [placed, flat(PARENTS)] + sizes(up) + [DMA((9,))],
-            (arrived, maps, filled) + up,
+            (slots, shape(*filled.shape), shape(*bank.shape, dtype=bf16)),
+            [VMEM] + [HBM] * 3,
+            (VMEM, HBM, HBM),
+            [maps_smem, pltpu.VMEM((CORNER, 16, 128), f32)] + split_wide + [placed, flat(PARENTS)] + up + [DMA((9,))],
+            (arrived, maps, filled, bank),
             600_000_000,
             "up",
+            {2: 1, 3: 2},
         )
         arrived = exchange(going)
-        corners.append(corner)
-        splits += [high, low]
     bases = call(
         base_kernel,
-        shape(3, *wide),
-        [HBM] * 10,
+        shape(13, *wide),
+        [HBM],
         HBM,
-        split_wide * 3 + sizes(both) + [pltpu.VMEM((3, *wide), f32), DMA((13,))],
-        tuple(splits) + both,
+        split_wide * 3 + both + [pltpu.VMEM((3, *wide), f32), DMA((13,))],
+        (bank,),
         7_200_000_000,
         "base",
+        limit=FULL,
     )
     height = levels - 1
     going = call(
         functools.partial(top_kernel, height),
         slots,
-        [VMEM] + [HBM] * 5,
+        [VMEM, HBM, HBM],
         VMEM,
-        [maps_smem] + split_wide + [placed, pltpu.VMEM(wide, f32), flat(PER)] + sizes(both) + [DMA((5,))],
-        (arrived, maps) + both,
+        [maps_smem] + split_wide + [placed, pltpu.VMEM(wide, f32), flat(PER)] + both + [DMA((5,))],
+        (arrived, maps, bank),
         2_400_000_000,
         "top",
     )
@@ -454,13 +495,13 @@
         going = call(
             functools.partial(down_kernel, height),
             slots,
-            [VMEM] + [HBM] * 7,
+            [VMEM] + [HBM] * 4,
             VMEM,
-            [maps_smem, pltpu.VMEM((320, 128), f32), pltpu.VMEM(wide, f32), pltpu.VMEM((8 * ROWS, 128), f32)]
+            [maps_smem, pltpu.VMEM((CORNER, 16, 128), f32), pltpu.VMEM(wide, f32), pltpu.VMEM((8 * ROWS, 128), f32)]
             + [pltpu.VMEM((320, 128), f32), pltpu.VMEM(wide, f32), flat(PER)]
-            + sizes(down)
+            + down
             + [DMA((7,))],
-            (returned, maps, corners[height], bases) + down,
+            (returned, maps, filled, bases, bank),
             800_000_000,
             "down",
         )

time: 344 us -> 328 us (0.953)
  local copies, waits for them, and re-layouts: 44.6 us -> 3.98 us
  waiting for transfers between devices: 40 us -> 57.1 us
  Pallas kernels: 63.2 us -> 71.6 us
    unnamed x120 -> x18, local copies, waits for them, and re-layouts: 44.6 us -> 3.98 us
    all_to_all x3, waiting for transfers between devices: 40 us -> 57.1 us  [exchange(): lax.all_to_all(blocks, 'dev', split_axis=0, concat_axis=0, tiled=True)]
    pallas_call x15, Pallas kernels: 63.2 us -> 71.6 us  [call(): pl.pallas_call(kernel, out_shape=out_shape, in_specs=in_specs, out_specs=...]
  transfers between devices with their start and end apart: 3 -> 3, of which waited for: 3 -> 3; matrix products, arithmetic and copies ran while one was open for 0% -> 0% of each run, Pallas kernels for 8% -> 10%
where the time goes in v1:
time: 328 us; the launch traced here: 327 us
  blocking collectives  172 us (52%)
  Pallas kernels  71.6 us (22%)
  waiting for transfers between devices  57.1 us (17%)
  starting transfers between devices  21.3 us (6%)
  local copies, waits for them, and re-layouts  3.98 us (1%)
    all_to_all x5, blocking collectives, exchange(): lax.all_to_all(blocks, 'dev', split_axis=0, concat_axis=0, tiled=True)  172 us
    pallas_call x15, Pallas kernels, call(): pl.pallas_call(kernel, out_shape=out_shape, in_specs=in_specs, out_specs=...  71.6 us
    all_to_all x3, waiting for transfers between devices, exchange(): lax.all_to_all(blocks, 'dev', split_axis=0, concat_axis=0, tiled=True)  57.1 us
    all_to_all x3, starting transfers between devices, exchange(): lax.all_to_all(blocks, 'dev', split_axis=0, concat_axis=0, tiled=True)  21.3 us
  transfers between devices with their start and end apart: 3, of which 3 were waited for; matrix products, arithmetic and copies ran while one was open for 0% of the time, Pallas kernels for 10%

profile of v1, /device:TPU:1, one launch (start us, length us, event | category | flops | bytes accessed | tf_op | source)
XLA Modules:
  0.0 327.2 jit_solution(11596653662635364286)
XLA Ops:
  0.0 3.0 pack_first.1
  3.0 0.0 copy-start.7
  3.0 11.5 %all-to-all-start = ((f32[256,16,128]{2,1,0:T(8,128)}), f32[256,16,128]{2,1,0:T(8,128)S(1)}, u32[]{:S(2)}, u32[]{:S(2)}) async-start(f32[256,16,128]{2,1,0:T(8,128)} %pack_first.1), calls=%async_computation | async-start | bytes 4194304 | tf_op jit(solution)/shard_map/all_to_all | solution.py:397
  14.5 0.2 select_reduce_fusion
  14.7 0.6 pad_add_fusion.maps.maps_ref
  15.4 5.0 %pack_rest.1.filled_ref = f32[8,276,16,128]{3,2,1,0:T(8,128)} custom-call(s32[8,128]{1,0:T(8,128)} %pad_add_fusion.maps.maps_ref, f32[2,464,1000]{2,1,0:T(8,128)} %bitcast.3), custom_call_target="tpu_custom_call" | custom-call | bytes 3716096 | tf_op jit(solution)/shard_map/pack_rest/pallas_call | solution.py:378
  20.3 11.8 %weights.1.bank_ref = bf16[16384,640]{1,0:T(8,128)(2,1)} custom-call(f32[20,20]{1,0:T(8,128)} %up_ref.1, f32[20,20]{1,0:T(8,128)} %down_ref.1), custom_call_target="tpu_custom_call" | custom-call | flops 50000000 | bytes 3200 | tf_op jit(solution)/shard_map/weights/pallas_call | solution.py:378
  32.2 12.9 %all-to-all-done.arrived_ref = f32[256,16,128]{2,1,0:T(8,128)S(1)} async-done(((f32[256,16,128]{2,1,0:T(8,128)}), f32[256,16,128]{2,1,0:T(8,128)S(1)}, u32[]{:S(2)}, u32[]{:S(2)}) %all-to-all-start) | async-done | bytes 2097184 | tf_op jit(solution)/shard_map/all_to_all | solution.py:397
  45.0 4.2 %up.3 = (f32[256,16,128]{2,1,0:T(8,128)S(1)}, f32[8,276,16,128]{3,2,1,0:T(8,128)}, bf16[16384,640]{1,0:T(8,128)(2,1)}) custom-call(f32[256,16,128]{2,1,0:T(8,128)S(1)} %all-to-all-done.arrived_ref, s32[8,128]{1,0:T(8,128)S(1)} %copy-done.6, f32[8,276,16,128]{3,2,1,0:T(8,128)} %pack_rest.1.filled_ref, ...), custom_call_target="tpu_custom_call", output_to_operand_aliasing={{1}: (2, {}), {2}: (3, {})} | custom-call | flops 600000000 | bytes 62132224 | tf_op jit(solution)/shard_map/up/pallas_call | solution.py:378
  49.3 34.4 %all_to_all.40.arrived_ref = f32[256,16,128]{2,1,0:T(8,128)S(1)} all-to-all(f32[256,16,128]{2,1,0:T(8,128)S(1)} %get-tuple-element.14), channel_id=1, replica_groups=mesh['dev'=128] {'dev'}, dimensions={0} | all-to-all | bytes 4194304 | tf_op jit(solution)/shard_map/all_to_all | solution.py:397
  83.7 4.2 %up.4 = (f32[256,16,128]{2,1,0:T(8,128)S(1)}, f32[8,276,16,128]{3,2,1,0:T(8,128)}, bf16[16384,640]{1,0:T(8,128)(2,1)}) custom-call(f32[256,16,128]{2,1,0:T(8,128)S(1)} %all_to_all.40.arrived_ref, s32[8,128]{1,0:T(8,128)S(1)} %copy-done.6, f32[8,276,16,128]{3,2,1,0:T(8,128)} %get-tuple-element.15.filled_ref, ...), custom_call_target="tpu_custom_call", output_to_operand_aliasing={{1}: (2, {}), {2}: (3, {})} | custom-call | flops 600000000 | bytes 62132224 | tf_op jit(solution)/shard_map/up/pallas_call | solution.py:378
  87.9 34.4 %all_to_all.41.arrived_ref = f32[256,16,128]{2,1,0:T(8,128)S(1)} all-to-all(f32[256,16,128]{2,1,0:T(8,128)S(1)} %get-tuple-element.17), channel_id=1, replica_groups=mesh['dev'=128] {'dev'}, dimensions={0} | all-to-all | bytes 4194304 | tf_op jit(solution)/shard_map/all_to_all | solution.py:397
  122.3 4.3 %up.5 = (f32[256,16,128]{2,1,0:T(8,128)S(1)}, f32[8,276,16,128]{3,2,1,0:T(8,128)}, bf16[16384,640]{1,0:T(8,128)(2,1)}) custom-call(f32[256,16,128]{2,1,0:T(8,128)S(1)} %all_to_all.41.arrived_ref, s32[8,128]{1,0:T(8,128)S(1)} %copy-done.6, f32[8,276,16,128]{3,2,1,0:T(8,128)} %get-tuple-element.18.filled_ref, ...), custom_call_target="tpu_custom_call", output_to_operand_aliasing={{1}: (2, {}), {2}: (3, {})} | custom-call | flops 600000000 | bytes 62132224 | tf_op jit(solution)/shard_map/up/pallas_call | solution.py:378
  126.5 34.4 %all_to_all.42.arrived_ref = f32[256,16,128]{2,1,0:T(8,128)S(1)} all-to-all(f32[256,16,128]{2,1,0:T(8,128)S(1)} %get-tuple-element.20), channel_id=1, replica_groups=mesh['dev'=128] {'dev'}, dimensions={0} | all-to-all | bytes 4194304 | tf_op jit(solution)/shard_map/all_to_all | solution.py:397
  160.9 5.4 %top.1 = f32[256,16,128]{2,1,0:T(8,128)S(1)} custom-call(f32[256,16,128]{2,1,0:T(8,128)S(1)} %all_to_all.42.arrived_ref, s32[8,128]{1,0:T(8,128)S(1)} %copy-done.6, bf16[16384,640]{1,0:T(8,128)(2,1)} %get-tuple-element.21.bank_ref), custom_call_target="tpu_custom_call" | custom-call | flops 2400000000 | bytes 44044288 | tf_op jit(solution)/shard_map/top/pallas_call | solution.py:378
  166.3 1.3 copy-done.4
  167.6 4.4 %all-to-all-start.4 = ((f32[256,16,128]{2,1,0:T(8,128)}), f32[256,16,128]{2,1,0:T(8,128)S(1)}, u32[]{:S(2)}, u32[]{:S(2)}) async-start(f32[256,16,128]{2,1,0:T(8,128)} %copy-done.4), calls=%async_computation.4 | async-start | bytes 4194304 | tf_op jit(solution)/shard_map/all_to_all | solution.py:397
  172.0 11.5 %base.1.base_ref = f32[13,640,512]{2,1,0:T(8,128)} custom-call(bf16[16384,640]{1,0:T(8,128)(2,1)} %get-tuple-element.21.bank_ref), custom_call_target="tpu_custom_call" | custom-call | flops 7200000000 | bytes 41943040 | tf_op jit(solution)/shard_map/base/pallas_call | solution.py:378
  183.5 19.2 %all-to-all-done.4.returned_ref = f32[256,16,128]{2,1,0:T(8,128)S(1)} async-done(((f32[256,16,128]{2,1,0:T(8,128)}), f32[256,16,128]{2,1,0:T(8,128)S(1)}, u32[]{:S(2)}, u32[]{:S(2)}) %all-to-all-start.4) | async-done | bytes 2097184 | tf_op jit(solution)/shard_map/all_to_all | solution.py:397
  202.7 4.4 %down.3 = f32[256,16,128]{2,1,0:T(8,128)S(1)} custom-call(f32[256,16,128]{2,1,0:T(8,128)S(1)} %all-to-all-done.4.returned_ref, s32[8,128]{1,0:T(8,128)S(1)} %copy-done.6, f32[8,276,16,128]{3,2,1,0:T(8,128)} %get-tuple-element.22.state_ref, f32[13,640,512]{2,1,0:T(8,128)} %base.1.base_ref, bf16[16384,640]{1,0:T(8,128)(2,1)} %get-tuple-element.21.bank_ref), custom_call_target="tpu_custom_call" | custom-call | flops 800000000 | bytes 79171584 | tf_op jit(solution)/shard_map/down/pallas_call | solution.py:378
  207.1 34.4 %all_to_all.43.returned_ref = f32[256,16,128]{2,1,0:T(8,128)S(1)} all-to-all(f32[256,16,128]{2,1,0:T(8,128)S(1)} %down.3), channel_id=1, replica_groups=mesh['dev'=128] {'dev'}, dimensions={0} | all-to-all | bytes 4194304 | tf_op jit(solution)/shard_map/all_to_all | solution.py:397
  241.5 5.1 %down.4 = f32[256,16,128]{2,1,0:T(8,128)S(1)} custom-call(f32[256,16,128]{2,1,0:T(8,128)S(1)} %all_to_all.43.returned_ref, s32[8,128]{1,0:T(8,128)S(1)} %copy-done.6, f32[8,276,16,128]{3,2,1,0:T(8,128)} %get-tuple-element.22.state_ref, f32[13,640,512]{2,1,0:T(8,128)} %base.1.base_ref, bf16[16384,640]{1,0:T(8,128)(2,1)} %get-tuple-element.21.bank_ref), custom_call_target="tpu_custom_call" | custom-call | flops 800000000 | bytes 79171584 | tf_op jit(solution)/shard_map/down/pallas_call | solution.py:378
  246.6 34.4 %all_to_all.44.returned_ref = f32[256,16,128]{2,1,0:T(8,128)S(1)} all-to-all(f32[256,16,128]{2,1,0:T(8,128)S(1)} %down.4), channel_id=1, replica_groups=mesh['dev'=128] {'dev'}, dimensions={0} | all-to-all | bytes 4194304 | tf_op jit(solution)/shard_map/all_to_all | solution.py:397
  281.0 4.4 %down.5 = f32[256,16,128]{2,1,0:T(8,128)S(1)} custom-call(f32[256,16,128]{2,1,0:T(8,128)S(1)} %all_to_all.44.returned_ref, s32[8,128]{1,0:T(8,128)S(1)} %copy-done.6, f32[8,276,16,128]{3,2,1,0:T(8,128)} %get-tuple-element.22.state_ref, f32[13,640,512]{2,1,0:T(8,128)} %base.1.base_ref, bf16[16384,640]{1,0:T(8,128)(2,1)} %get-tuple-element.21.bank_ref), custom_call_target="tpu_custom_call" | custom-call | flops 800000000 | bytes 79171584 | tf_op jit(solution)/shard_map/down/pallas_call | solution.py:378
  285.3 1.3 copy-done.2
  286.7 1.3 copy-done.5
  288.0 5.4 %all-to-all-start.7 = ((f32[256,16,128]{2,1,0:T(8,128)}), f32[256,16,128]{2,1,0:T(8,128)}, u32[]{:S(2)}, u32[]{:S(2)}) async-start(f32[256,16,128]{2,1,0:T(8,128)} %copy-done.5), calls=%async_computation.7 | async-start | bytes 4194304 | tf_op jit(solution)/shard_map/all_to_all | solution.py:397
  293.4 1.7 store.4.rest_0_
  295.2 1.7 store.5.rest_0_
  296.9 1.7 store.6.rest_0_
  298.6 25.1 %all-to-all-done.7.returned_ref = f32[256,16,128]{2,1,0:T(8,128)} async-done(((f32[256,16,128]{2,1,0:T(8,128)}), f32[256,16,128]{2,1,0:T(8,128)}, u32[]{:S(2)}, u32[]{:S(2)}) %all-to-all-start.7) | async-done | bytes 2097184 | tf_op jit(solution)/shard_map/all_to_all | solution.py:397
  323.7 3.3 %store.7 = f32[2,464,1000]{2,1,0:T(8,128)} custom-call(f32[256,16,128]{2,1,0:T(8,128)} %all-to-all-done.7.returned_ref, s32[8,128]{1,0:T(8,128)S(1)} %copy-done.6, f32[2,464,1000]{2,1,0:T(8,128)} %store.6.rest_0_), custom_call_target="tpu_custom_call", output_to_operand_aliasing={{}: (2, {})} | custom-call | bytes 5813248 | tf_op jit(solution)/shard_map/store/pallas_call | solution.py:378
  (14 shorter events, 0.0 us)
Async XLA Ops:
  3.0 11.5 %copy-start.7 = (s32[4,256]{1,0:T(4,128)S(1)}, s32[4,256]{1,0:T(4,128)}, u32[]{:S(2)}) copy-start(s32[4,256]{1,0:T(4,128)} %send_ref.1) | copy-start | bytes 12292
  3.0 11.5 %copy-start.8 = (s32[4,256]{1,0:T(4,128)S(1)}, s32[4,256]{1,0:T(4,128)}, u32[]{:S(2)}) copy-start(s32[4,256]{1,0:T(4,128)} %param.7) | copy-start | bytes 12292
  3.0 42.0 %all-to-all-start = ((f32[256,16,128]{2,1,0:T(8,128)}), f32[256,16,128]{2,1,0:T(8,128)S(1)}, u32[]{:S(2)}, u32[]{:S(2)}) async-start(f32[256,16,128]{2,1,0:T(8,128)} %pack_first.1), calls=%async_computation | async-start | bytes 4194304 | tf_op jit(solution)/shard_map/all_to_all | solution.py:397
  20.3 24.7 %copy-start.6 = (s32[8,128]{1,0:T(8,128)S(1)}, s32[8,128]{1,0:T(8,128)}, u32[]{:S(2)}) copy-start(s32[8,128]{1,0:T(8,128)} %pad_add_fusion.maps.maps_ref) | copy-start | bytes 12292
  166.3 1.3 copy-start.4
  167.6 35.0 %all-to-all-start.4 = ((f32[256,16,128]{2,1,0:T(8,128)}), f32[256,16,128]{2,1,0:T(8,128)S(1)}, u32[]{:S(2)}, u32[]{:S(2)}) async-start(f32[256,16,128]{2,1,0:T(8,128)} %copy-done.4), calls=%async_computation.4 | async-start | bytes 4194304 | tf_op jit(solution)/shard_map/all_to_all | solution.py:397
  241.4 5.1 %copy-start = (f32[256,16,128]{2,1,0:T(8,128)}, f32[256,16,128]{2,1,0:T(8,128)S(1)}, u32[]{:S(2)}) copy-start(f32[256,16,128]{2,1,0:T(8,128)S(1)} %all_to_all.43.returned_ref) | copy-start | bytes 6291460
  285.3 1.3 copy-start.2
  286.7 1.3 copy-start.5
  288.0 35.8 %all-to-all-start.7 = ((f32[256,16,128]{2,1,0:T(8,128)}), f32[256,16,128]{2,1,0:T(8,128)}, u32[]{:S(2)}, u32[]{:S(2)}) async-start(f32[256,16,128]{2,1,0:T(8,128)} %copy-done.5), calls=%async_computation.7 | async-start | bytes 4194304 | tf_op jit(solution)/shard_map/all_to_all | solution.py:397
  293.4 1.8 copy-start.1
  295.2 1.7 copy-start.3
